TPU v7x, 512 devices: a whole 4x4x16 slice. The times are simulated.
512 devices in a mesh: chan: 64 (over x, z_lo, core), stn: 8 (over y, z_hi).
Axes of the slice: x: 4, y: 4, z: 16 (z_hi: 2, z_lo: 8; z = z_hi * 8 + z_lo), core: 2. Of those that a mesh axis runs over, the one named last changes fastest.
Arguments:
- voltages: bfloat16 [2, 512, 524288], P(None, 'stn', 'chan'), may hold values from -12 to 12
Outputs:
- visibilities: bfloat16 [2048, 512, 5, 128], P('chan', 'stn')
All inputs are finite; a program needn't handle non-finite values.
Results may differ from a plain program's by a relative error of at most 0.0031.
Values may be sent and summed in bfloat16 or wider, within the bound.
A program may use at most 64 MiB of HBM per device.

v0:
```python
import math

import jax
import jax.numpy as jnp
from jax import lax
from jax.sharding import PartitionSpec as P

NCH = 2048
RADIX = 32
TAPS = 4


def from_behind(array, axis, by):
    count = lax.axis_size(axis)
    pairs = [(i, i + by) for i in range(count) if 0 <= i + by < count]
    return lax.ppermute(array, axis, pairs)


def shifted(array, axis, by):
    count = lax.axis_size(axis)
    return lax.ppermute(array, axis, [(i, (i + by) % count) for i in range(count)])


def prototype(tap_count, chan_count):
    position = jnp.arange(tap_count * chan_count, dtype=jnp.float32) + 0.5
    centered = (position - tap_count * chan_count / 2.0) / chan_count
    window = 0.5 - 0.5 * jnp.cos(2.0 * math.pi * position / (tap_count * chan_count))
    return (jnp.sinc(centered) * window).reshape(tap_count, chan_count)


def phase_table(rows_len, cols_len, modulus):
    row_index = jnp.arange(rows_len, dtype=jnp.int32)
    col_index = jnp.arange(cols_len, dtype=jnp.int32)
    product = row_index[:, None] * col_index[None, :] % modulus
    angles = -2.0 * math.pi / modulus * product.astype(jnp.float32)
    return (jnp.cos(angles), jnp.sin(angles))


def block_table(cos_part, sin_part):
    from_real = jnp.stack([cos_part, sin_part], axis=1)
    from_imag = jnp.stack([-sin_part, cos_part], axis=1)
    return jnp.stack([from_real, from_imag], axis=0)


def channelize(filtered, first_len):
    inputs_here, spectra_here, total_len = filtered.shape[1:]
    second_len = total_len // first_len
    cos_one, sin_one = phase_table(first_len, first_len, first_len)
    cos_two, sin_two = phase_table(second_len, second_len, second_len)
    cos_tw, sin_tw = phase_table(first_len, second_len, total_len)
    shaped = filtered.reshape(2, inputs_here, spectra_here, first_len, second_len)
    section = jnp.einsum(
        "xpsab,xayk->ypskb", shaped, block_table(cos_one, sin_one), precision=lax.Precision.HIGH
    )
    turned_re = section[0] * cos_tw - section[1] * sin_tw
    turned_im = section[0] * sin_tw + section[1] * cos_tw
    turned = jnp.stack([turned_re, turned_im], axis=0)
    final = jnp.einsum(
        "ypskb,ybzm->mkszp", turned, block_table(cos_two, sin_two), precision=lax.Precision.HIGH
    )
    norm_scale = total_len ** (-0.5)
    return final.reshape(total_len, spectra_here, 2 * inputs_here) * norm_scale


def split_parts(products, half):
    real_part = products[..., :half, :half] + products[..., half:, half:]
    imag_part = products[..., half:, :half] - products[..., :half, half:]
    return (real_part, imag_part)


def correlate(own_block, partner, norm_scale):
    products = (
        jnp.einsum("csa,csb->cab", own_block, partner, preferred_element_type=jnp.float32)
        * norm_scale
    )
    return split_parts(products, own_block.shape[2] // 2)


def local(voltages):
    inputs_here = voltages.shape[1]
    per_dev = voltages.shape[2] // NCH
    carried = from_behind(voltages[:, :, (per_dev - TAPS + 1) * NCH :], "chan", 1)
    extended = jnp.concatenate([carried, voltages], axis=2)
    extended = extended.reshape(2, inputs_here, per_dev + TAPS - 1, NCH).astype(jnp.float32)
    weights = prototype(TAPS, NCH)
    filtered = weights[0] * extended[:, :, 0:per_dev]
    for tap_index in range(1, TAPS):
        filtered = filtered + weights[tap_index] * extended[:, :, tap_index : tap_index + per_dev]
    spectra = channelize(filtered, RADIX).astype(jnp.bfloat16)
    turned = lax.all_to_all(spectra, "chan", split_axis=0, concat_axis=1, tiled=True)
    spectra_all = turned.shape[1]
    norm_scale = 1.0 / spectra_all
    stations = lax.axis_size("stn")
    lag_count = stations // 2 + 1
    pieces = [correlate(turned, turned, norm_scale)]
    partner = turned
    for lag_index in range(1, lag_count):
        partner = shifted(partner, "stn", -1)
        pieces.append(correlate(turned, partner, norm_scale))
    real_all = jnp.stack([piece[0] for piece in pieces], axis=2)
    imag_all = jnp.stack([piece[1] for piece in pieces], axis=2)
    return jnp.concatenate([real_all, imag_all], axis=3).astype(jnp.bfloat16)


def solution(mesh):
    return jax.shard_map(
        local,
        mesh=mesh,
        in_specs=(P(None, "stn", "chan"),),
        out_specs=P("chan", "stn", None, None),
        check_vma=False,
    )
```

profile of v0, /device:TPU:1, one launch (start us, length us, event | category | flops | bytes accessed | tf_op | source)
XLA Modules:
  0.0 963.2 jit_solution(6319470655099886618)
XLA Ops:
  0.0 0.0 copy-start
  0.0 1.7 slice.100
  1.7 4.9 collective-permute-start
  6.6 0.1 fusion.104
  6.7 0.2 fusion.54
  6.9 0.1 fusion.102
  7.0 0.1 fusion.100
  7.1 0.1 fusion.99
  7.2 0.1 fusion.95
  7.4 16.5 %collective-permute-done = bf16[2,64,6144]{2,1,0:T(8,128)(2,1)S(1)} collective-permute-done((bf16[2,64,6144]{2,1,0:T(8,128)(2,1)S(1)}, bf16[2,64,6144]{2,1,0:T(8,128)(2,1)S(1)}, u32[]{:S(2)}, u32[]{:S(2)}) %collective-permute-start) | collective-permute-done | bytes 1572896 | tf_op jit(solution)/shard_map/ppermute | solution.py:16
  24.0 0.0 copy-done
  24.0 3.7 maximum_convert_fusion
  27.7 9.6 reshape.210
  37.3 15.0 %fusion.8 = f32[2,64,4,2048]{3,2,1,0:T(4,128)} fusion(f32[2,64,7,2048]{3,2,1,0:T(8,128)} %reshape.210, f32[2048]{0:T(1024)S(1)} %get-tuple-element.20, f32[2048]{0:T(1024)S(1)} %get-tuple-element.21, f32[2048]{0:T(1024)S(1)} %get-tuple-element.22, f32[2048]{0:T(1024)S(1)} %get-tuple-element.19), kind=kLoop, calls=%fused_computation.11 | loop fusion | flops 7340032 | bytes 21004288 | tf_op jit(solution)/shard_map/add | solution.py:88
  52.3 8.2 reshape.209
  60.5 6.4 fusion.11
  66.8 2.0 multiply_subtract_fusion
  68.9 2.0 pad_maximum_fusion
  70.8 9.6 fusion.7
  80.4 6.3 copy.47
  86.7 7.5 reshape.217
  94.2 112.3 %all_to_all.18 = bf16[2048,4,128]{2,1,0:T(4,128)(2,1)S(1)} all-to-all(bf16[2048,4,128]{2,1,0:T(4,128)(2,1)S(1)} %reshape.217), channel_id=1, replica_groups=mesh['chan'=64,'stn'=8] {'chan'}, dimensions={0} | all-to-all | bytes 4194304 | tf_op jit(solution)/shard_map/all_to_all | solution.py:90
  206.4 0.3 copy.30
  206.7 1.6 copy.31
  208.3 14.7 %collective-permute-start.1 = (bf16[32,256,128]{2,1,0:T(8,128)(2,1)S(1)}, bf16[32,256,128]{2,1,0:T(8,128)(2,1)S(1)}, u32[]{:S(2)}, u32[]{:S(2)}) collective-permute-start(bf16[32,256,128]{2,1,0:T(8,128)(2,1)S(1)} %bitcast.100), channel_id=1, source_target_pairs={{0,7},{1,0},{2,1},{3,2},{4,3},{5,4},{6,5},{7,6},{8,15},{9,8},{10,9... | collective-permute-start | bytes 6291464 | tf_op jit(solution)/shard_map/ppermute | solution.py:21
  223.0 175.5 %collective-permute-done.1 = bf16[32,256,128]{2,1,0:T(8,128)(2,1)S(1)} collective-permute-done((bf16[32,256,128]{2,1,0:T(8,128)(2,1)S(1)}, bf16[32,256,128]{2,1,0:T(8,128)(2,1)S(1)}, u32[]{:S(2)}, u32[]{:S(2)}) %collective-permute-start.1) | collective-permute-done | bytes 2097184 | tf_op jit(solution)/shard_map/ppermute | solution.py:21
  398.6 14.8 %collective-permute-start.2 = (bf16[32,256,128]{2,1,0:T(8,128)(2,1)S(1)}, bf16[32,256,128]{2,1,0:T(8,128)(2,1)S(1)}, u32[]{:S(2)}, u32[]{:S(2)}) collective-permute-start(bf16[32,256,128]{2,1,0:T(8,128)(2,1)S(1)} %collective-permute-done.1), channel_id=1, source_target_pairs={{0,7},{1,0},{2,1},{3,2},{4,3},{5,4},{6,5},{7,6},{8,15},{9,8},{10,9... | collective-permute-start | bytes 6291464 | tf_op jit(solution)/shard_map/ppermute | solution.py:21
  413.4 177.9 %collective-permute-done.2 = bf16[32,256,128]{2,1,0:T(8,128)(2,1)S(1)} collective-permute-done((bf16[32,256,128]{2,1,0:T(8,128)(2,1)S(1)}, bf16[32,256,128]{2,1,0:T(8,128)(2,1)S(1)}, u32[]{:S(2)}, u32[]{:S(2)}) %collective-permute-start.2) | collective-permute-done | bytes 2097184 | tf_op jit(solution)/shard_map/ppermute | solution.py:21
  591.3 10.0 %collective-permute-start.3 = (bf16[32,256,128]{2,1,0:T(8,128)(2,1)S(1)}, bf16[32,256,128]{2,1,0:T(8,128)(2,1)S(1)}, u32[]{:S(2)}, u32[]{:S(2)}) collective-permute-start(bf16[32,256,128]{2,1,0:T(8,128)(2,1)S(1)} %collective-permute-done.2), channel_id=1, source_target_pairs={{0,7},{1,0},{2,1},{3,2},{4,3},{5,4},{6,5},{7,6},{8,15},{9,8},{10,9... | collective-permute-start | bytes 6291464 | tf_op jit(solution)/shard_map/ppermute | solution.py:21
  601.3 0.8 convolution_multiply_fusion.4
  602.1 174.3 %collective-permute-done.3 = bf16[32,256,128]{2,1,0:T(8,128)(2,1)S(1)} collective-permute-done((bf16[32,256,128]{2,1,0:T(8,128)(2,1)S(1)}, bf16[32,256,128]{2,1,0:T(8,128)(2,1)S(1)}, u32[]{:S(2)}, u32[]{:S(2)}) %collective-permute-start.3) | collective-permute-done | bytes 2097184 | tf_op jit(solution)/shard_map/ppermute | solution.py:21
  776.3 8.2 collective-permute-start.4
  784.5 0.6 fusion.27
  785.1 0.8 convolution_multiply_fusion.3
  785.9 0.8 fusion.29
  786.8 0.8 convolution_multiply_fusion.2
  787.6 0.8 fusion.31
  788.4 0.8 convolution_multiply_fusion.1
  789.1 0.8 fusion.33
  790.0 168.1 %collective-permute-done.4 = bf16[32,256,128]{2,1,0:T(8,128)(2,1)S(1)} collective-permute-done((bf16[32,256,128]{2,1,0:T(8,128)(2,1)S(1)}, bf16[32,256,128]{2,1,0:T(8,128)(2,1)S(1)}, u32[]{:S(2)}, u32[]{:S(2)}) %collective-permute-start.4) | collective-permute-done | bytes 2097184 | tf_op jit(solution)/shard_map/ppermute | solution.py:21
  958.1 0.8 convolution_multiply_fusion
  958.8 0.8 fusion.35
  959.7 1.5 pad_maximum_fusion.1
  961.1 2.0 copy.37
  (3 shorter events, 0.0 us)
Async XLA Ops:
  0.0 24.0 %copy-start = (bf16[2,64,8192]{2,1,0:T(8,128)(2,1)S(1)}, bf16[2,64,8192]{2,1,0:T(8,128)(2,1)}, u32[]{:S(2)}) copy-start(bf16[2,64,8192]{2,1,0:T(8,128)(2,1)} %param.1) | copy-start | bytes 6291460
  1.7 22.3 %collective-permute-start = (bf16[2,64,6144]{2,1,0:T(8,128)(2,1)S(1)}, bf16[2,64,6144]{2,1,0:T(8,128)(2,1)S(1)}, u32[]{:S(2)}, u32[]{:S(2)}) collective-permute-start(bf16[2,64,6144]{2,1,0:T(8,128)(2,1)S(1)} %slice.100), channel_id=1, source_target_pairs={{0,8},{8,16},{16,24},{24,32},{32,40},{40,48},{48,56},{56,64},{64,7... | collective-permute-start | bytes 4718600 | tf_op jit(solution)/shard_map/ppermute | solution.py:16
  208.3 190.2 %collective-permute-start.1 = (bf16[32,256,128]{2,1,0:T(8,128)(2,1)S(1)}, bf16[32,256,128]{2,1,0:T(8,128)(2,1)S(1)}, u32[]{:S(2)}, u32[]{:S(2)}) collective-permute-start(bf16[32,256,128]{2,1,0:T(8,128)(2,1)S(1)} %bitcast.100), channel_id=1, source_target_pairs={{0,7},{1,0},{2,1},{3,2},{4,3},{5,4},{6,5},{7,6},{8,15},{9,8},{10,9... | collective-permute-start | bytes 6291464 | tf_op jit(solution)/shard_map/ppermute | solution.py:21
  398.6 192.7 %collective-permute-start.2 = (bf16[32,256,128]{2,1,0:T(8,128)(2,1)S(1)}, bf16[32,256,128]{2,1,0:T(8,128)(2,1)S(1)}, u32[]{:S(2)}, u32[]{:S(2)}) collective-permute-start(bf16[32,256,128]{2,1,0:T(8,128)(2,1)S(1)} %collective-permute-done.1), channel_id=1, source_target_pairs={{0,7},{1,0},{2,1},{3,2},{4,3},{5,4},{6,5},{7,6},{8,15},{9,8},{10,9... | collective-permute-start | bytes 6291464 | tf_op jit(solution)/shard_map/ppermute | solution.py:21
  591.3 185.1 %collective-permute-start.3 = (bf16[32,256,128]{2,1,0:T(8,128)(2,1)S(1)}, bf16[32,256,128]{2,1,0:T(8,128)(2,1)S(1)}, u32[]{:S(2)}, u32[]{:S(2)}) collective-permute-start(bf16[32,256,128]{2,1,0:T(8,128)(2,1)S(1)} %collective-permute-done.2), channel_id=1, source_target_pairs={{0,7},{1,0},{2,1},{3,2},{4,3},{5,4},{6,5},{7,6},{8,15},{9,8},{10,9... | collective-permute-start | bytes 6291464 | tf_op jit(solution)/shard_map/ppermute | solution.py:21
  776.3 181.7 %collective-permute-start.4 = (bf16[32,256,128]{2,1,0:T(8,128)(2,1)S(1)}, bf16[32,256,128]{2,1,0:T(8,128)(2,1)S(1)}, u32[]{:S(2)}, u32[]{:S(2)}) collective-permute-start(bf16[32,256,128]{2,1,0:T(8,128)(2,1)S(1)} %collective-permute-done.3), channel_id=1, source_target_pairs={{0,7},{1,0},{2,1},{3,2},{4,3},{5,4},{6,5},{7,6},{8,15},{9,8},{10,9... | collective-permute-start | bytes 6291464 | tf_op jit(solution)/shard_map/ppermute | solution.py:21
where the time goes:
time: 969 us; the launch traced here: 963 us
  waiting for transfers between devices  712 us (73%)
  blocking collectives  112 us (12%)
  starting transfers between devices  52.7 us (5%)
  local copies, waits for them, and re-layouts  37.1 us (4%)
  other arithmetic  28.8 us (3%)
  matrix products  19.8 us (2%)
    ppermute x4, waiting for transfers between devices, shifted(): lax.ppermute(array, axis, [(i, (i + by) % count) for i in range(count)])  696 us
    all_to_all x1, blocking collectives, local(): lax.all_to_all(spectra, 'chan', split_axis=0, concat_axis=1, tiled=True)  112 us
    ppermute x4, starting transfers between devices, shifted(): lax.ppermute(array, axis, [(i, (i + by) % count) for i in range(count)])  47.7 us
  transfers between devices with their start and end apart: 5, of which 5 were waited for; matrix products, arithmetic and copies ran while one was open for 1% of the time, Pallas kernels for 0%

commit v1 on v0

v1 whole, which is shorter than its diff:
```python
import math

import jax
import jax.numpy as jnp
import numpy as np
from jax import lax
from jax.experimental import pallas as pl
from jax.experimental.pallas import tpu as pltpu
from jax.sharding import PartitionSpec as P

MESH = pl.DeviceIdType.MESH
NCH = 2048
TAPS = 4
SPEC = 4
RAD = 16
LEN = 128
IN_DEV = 64
NX, NZL, NCORE, NY, NZH = 4, 8, 2, 4, 2
NXC = NX * NCORE
PLANE = NXC * NY
NZ = NZL * NZH
CHAN = NX * NZL * NCORE
STN = NY * NZH
LAGS = STN // 2 + 1
KK = RAD // NY
CHUNKS = 2 * KK
BF = jnp.bfloat16
F32 = jnp.float32


def tables():
    position = np.arange(TAPS * NCH, dtype=np.float64) + 0.5
    centered = (position - TAPS * NCH / 2.0) / NCH
    window = 0.5 - 0.5 * np.cos(2.0 * math.pi * position / (TAPS * NCH))
    weights = (np.sinc(centered) * window).reshape(TAPS * RAD, LEN).astype(np.float32)
    angle = 2.0 * math.pi / NCH * np.outer(np.arange(RAD), np.arange(LEN))
    twiddle = np.concatenate([np.cos(angle), np.sin(angle)], axis=0).astype(np.float32)
    x, core, zl, half = np.meshgrid(
        np.arange(NX), np.arange(NCORE), np.arange(NZL), np.arange(2), indexing="ij"
    )
    order = (((x * NZL + zl) * NCORE + core) * 2 + half).reshape(-1)
    angle = 2.0 * math.pi / LEN * (np.outer(order, np.arange(LEN)) % LEN)
    table = np.concatenate([np.cos(angle), np.sin(angle)], axis=1) * NCH**-0.5
    high = table.astype(np.float32).astype(BF)
    low = (table - high.astype(np.float64)).astype(np.float32).astype(BF)
    swap = np.zeros((16, 16, 16, 16), np.float32)
    for t in range(16):
        for j in range(16):
            swap[j, t, t, j] = 1.0
    swap = swap.reshape(256, 256).astype(BF)
    return weights, twiddle, high, low, swap


def transform(points):
    count = len(points)
    if count == 1:
        return points
    even, odd = transform(points[0::2]), transform(points[1::2])
    low, high = [], []
    for k in range(count // 2):
        re, im = odd[k]
        if k == 0:
            pass
        elif 4 * k == count:
            re, im = im, -re
        elif 8 * k == count:
            re, im = (re + im) * math.sqrt(0.5), (im - re) * math.sqrt(0.5)
        elif 8 * k == 3 * count:
            re, im = (im - re) * math.sqrt(0.5), (re + im) * -math.sqrt(0.5)
        else:
            c, s = math.cos(2 * math.pi * k / count), math.sin(2 * math.pi * k / count)
            re, im = re * c + im * s, im * c - re * s
        low.append((even[k][0] + re, even[k][1] + im))
        high.append((even[k][0] - re, even[k][1] - im))
    return low + high


def kernel(
    x_ref, wts_ref, tw_ref, ah_ref, al_ref, swap_ref, out_ref,
    halo, yh, yl, b1, r1, zs, zr, gw, ob,
    halo_send, halo_recv, xy_send, xy_recv, z_send, z_recv, o_send, o_recv,
):
    chan, stn = lax.axis_index("chan"), lax.axis_index("stn")
    core = chan % NCORE
    zl = (chan // NCORE) % NZL
    x = chan // (NCORE * NZL)
    y, zh = stn // NZH, stn % NZH
    me_xy = y * NXC + x * NCORE + core
    me_z = zh * NZL + zl

    def at_xy(i):
        xc = i % NXC
        return {"chan": ((xc // NCORE) * NZL + zl) * NCORE + xc % NCORE, "stn": (i // NXC) * NZH + zh}

    def at_z(i):
        return {"chan": (x * NZL + i % NZL) * NCORE + core, "stn": y * NZH + i // NZL}

    after = {"chan": (chan + 1) % CHAN, "stn": stn}
    before = {"chan": (chan + CHAN - 1) % CHAN, "stn": stn}

    barrier = pltpu.get_barrier_semaphore()

    def greet(device):
        pl.semaphore_signal(barrier, inc=1, device_id=device, device_id_type=MESH)

    greet(after)
    greet(before)

    @pl.loop(1, PLANE)
    def _(j):
        greet(at_xy((me_xy + j) % PLANE))

    @pl.loop(1, NZ)
    def _(j):
        greet(at_z((me_z + j) % NZ))

    pl.semaphore_wait(barrier, PLANE + NZ)

    def send_halo(block, slot):
        pltpu.make_async_remote_copy(
            src_ref=x_ref.at[:, :, pl.ds(block * NCH, NCH)],
            dst_ref=halo.at[slot],
            send_sem=halo_send.at[slot],
            recv_sem=halo_recv.at[slot],
            device_id=after,
            device_id_type=MESH,
        ).start()

    def wait_halo(slot):
        pltpu.make_async_copy(halo.at[slot], halo.at[slot], halo_recv.at[slot]).wait()

    send_halo(3, 2)
    send_halo(2, 1)
    send_halo(1, 0)
    valid = (chan > 0).astype(F32)

    def spectrum(s):
        @pl.loop(0, IN_DEV // 16)
        def _(tile):
            rows = pl.ds(pl.multiple_of(tile * 16, 16), 16)
            points = []
            for a in range(RAD):
                pair = []
                for part in range(2):
                    here = there = None
                    for tap in range(TAPS):
                        w = wts_ref[pl.ds(tap * RAD + a, 1), :]
                        j = s - 3 + tap
                        if j >= 0:
                            v = x_ref[part, rows, pl.ds(j * NCH + a * LEN, LEN)].astype(F32) * w
                            here = v if here is None else here + v
                        else:
                            v = halo[3 + j, part, rows, pl.ds(a * LEN, LEN)].astype(F32) * w
                            there = v if there is None else there + v
                    pair.append(here if there is None else here + there * valid)
                points.append(tuple(pair))
            turned = transform(points)
            low_rows = pl.ds(pl.multiple_of(IN_DEV + tile * 16, 16), 16)
            for k in range(RAD):
                re, im = turned[k]
                if k > 0:
                    c, sn = tw_ref[pl.ds(k, 1), :], tw_ref[pl.ds(RAD + k, 1), :]
                    re, im = re * c + im * sn, im * c - re * sn
                re_h, im_h = re.astype(BF), im.astype(BF)
                re_l = (re - re_h.astype(F32)).astype(BF)
                im_l = (im - im_h.astype(F32)).astype(BF)
                for ref, r, i in ((yh, re_h, im_h), (yl, re_l, im_l)):
                    ref[s % 2, k, rows, 0:LEN] = r
                    ref[s % 2, k, rows, LEN : 2 * LEN] = i
                    ref[s % 2, k, low_rows, 0:LEN] = i
                    ref[s % 2, k, low_rows, LEN : 2 * LEN] = -r

    def dot_nt(a, b):
        return lax.dot_general(a, b, (((1,), (1,)), ((), ())), preferred_element_type=F32)

    def channels(chunk, kk):
        @pl.loop(0, NY)
        def _(yd):
            k = yd * KK + kk
            for s in range(2):
                high, low = yh[s, k], yl[s, k]
                o = dot_nt(ah_ref[...], high) + dot_nt(al_ref[...], high) + dot_nt(ah_ref[...], low)
                b1[chunk, pl.ds(yd * NXC, NXC), s] = o.astype(BF).reshape(NXC, 16, LEN)

        pltpu.make_async_copy(b1.at[chunk, me_xy], r1.at[chunk, me_xy], xy_recv.at[chunk]).start()

        @pl.loop(1, PLANE)
        def _(j):
            to = (me_xy + j) % PLANE
            pltpu.make_async_remote_copy(
                src_ref=b1.at[chunk, to],
                dst_ref=r1.at[chunk, me_xy],
                send_sem=xy_send,
                recv_sem=xy_recv.at[chunk],
                device_id=at_xy(to),
                device_id_type=MESH,
            ).start()

    def spread(chunk):
        pltpu.make_async_copy(r1.at[chunk], r1.at[chunk], xy_recv.at[chunk]).wait()

        @pl.loop(0, NY)
        def _(yd):
            rows = r1[chunk, pl.ds(yd * NXC, NXC)].reshape(256, LEN)
            o = jnp.dot(swap_ref[...], rows, preferred_element_type=F32).astype(BF)
            zs[chunk, :, :, yd] = o.reshape(NZL, 2, 16, LEN)

        pltpu.make_async_copy(zs.at[chunk, zl], zr.at[chunk, me_z], z_recv.at[chunk]).start()

        @pl.loop(1, NZ)
        def _(j):
            to = (me_z + j) % NZ
            pltpu.make_async_remote_copy(
                src_ref=zs.at[chunk, to % NZL],
                dst_ref=zr.at[chunk, me_z],
                send_sem=z_send,
                recv_sem=z_recv.at[chunk],
                device_id=at_z(to),
                device_id_type=MESH,
            ).start()

    def phase(base):
        channels(base, 0)

        @pl.loop(1, KK)
        def _(kk):
            channels(base + kk, kk)
            spread(base + kk - 1)

        spread(base + KK - 1)

    spectrum(3)
    wait_halo(2)
    spectrum(2)
    phase(0)
    wait_halo(1)
    spectrum(1)
    wait_halo(0)
    spectrum(0)
    phase(KK)

    lane = lax.broadcasted_iota(jnp.int32, (IN_DEV, LEN), 1)
    scale = 1.0 / (CHAN * SPEC)
    sign = jnp.where(lane < IN_DEV, scale, -scale).astype(F32)

    @pl.loop(0, KK)
    def _(kk):
        for base in (0, KK):
            pltpu.make_async_copy(zr.at[base + kk], zr.at[base + kk], z_recv.at[base + kk]).wait()

        @pl.loop(0, 2)
        def _(half):
            for g in range(STN + LAGS - 1):
                st = (zh + g) % STN
                for sp in range(2):
                    part = zr[sp * KK + kk, pl.ds((st % NZH) * NZL, NZL), half, st // NZH]
                    gw[pl.ds(sp * 128, 128), pl.ds(g * LEN, LEN)] = part.reshape(128, LEN)
            slot = half * KK + kk
            for yo in range(NY):
                own = gw[:, pl.ds(2 * yo * LEN, LEN)]
                partner = gw[:, pl.ds(2 * yo * LEN, LAGS * LEN)]
                prod = lax.dot_general(
                    own, partner, (((0,), (0,)), ((), ())), preferred_element_type=F32
                )
                for lag in range(LAGS):
                    top = prod[:IN_DEV, lag * LEN : (lag + 1) * LEN]
                    low = prod[IN_DEV:, lag * LEN : (lag + 1) * LEN]
                    both = top * sign + pltpu.roll(low, IN_DEV, 1) * scale
                    ob[slot, yo, lag] = both.astype(BF)
            ch = half * RAD + y * KK + kk
            pltpu.make_async_copy(ob.at[slot, y], out_ref.at[ch], o_recv).start()

            @pl.loop(1, NY)
            def _(j):
                to = (y + j) % NY
                pltpu.make_async_remote_copy(
                    src_ref=ob.at[slot, to],
                    dst_ref=out_ref.at[ch],
                    send_sem=o_send,
                    recv_sem=o_recv,
                    device_id={"chan": chan, "stn": to * NZH + zh},
                    device_id_type=MESH,
                ).start()

    pltpu.make_async_copy(out_ref, out_ref, o_recv).wait()
    for slot in range(3):
        pltpu.make_async_copy(halo.at[slot], halo.at[slot], halo_send.at[slot]).wait()
    sent = b1.at[:, pl.ds(0, PLANE - 1)]
    pltpu.make_async_copy(sent, sent, xy_send).wait()
    sent = zr.at[:, pl.ds(0, NZ - 1)]
    pltpu.make_async_copy(sent, sent, z_send).wait()
    sent = ob.at[:, pl.ds(0, NY - 1)]
    pltpu.make_async_copy(sent, sent, o_send).wait()


def local(voltages):
    vmem = pl.BlockSpec(memory_space=pltpu.VMEM)
    dma = pltpu.SemaphoreType.DMA
    products = pl.pallas_call(
        kernel,
        out_shape=jax.ShapeDtypeStruct((2 * RAD, LAGS, IN_DEV, LEN), BF),
        in_specs=[vmem] * 6,
        out_specs=pl.BlockSpec(memory_space=pl.ANY),
        scratch_shapes=[
            pltpu.VMEM((3, 2, IN_DEV, NCH), BF),
            pltpu.VMEM((2, RAD, 2 * IN_DEV, 2 * LEN), BF),
            pltpu.VMEM((2, RAD, 2 * IN_DEV, 2 * LEN), BF),
            pltpu.VMEM((CHUNKS, PLANE, 2, 16, LEN), BF),
            pltpu.VMEM((CHUNKS, PLANE, 2, 16, LEN), BF),
            pltpu.VMEM((CHUNKS, NZL, 2, NY, 16, LEN), BF),
            pltpu.VMEM((CHUNKS, NZ, 2, NY, 16, LEN), BF),
            pltpu.VMEM((256, (STN + LAGS - 1) * LEN), BF),
            pltpu.VMEM((2 * KK, NY, LAGS, IN_DEV, LEN), BF),
            dma((3,)),
            dma((3,)),
            dma,
            dma((CHUNKS,)),
            dma,
            dma((CHUNKS,)),
            dma,
            dma,
        ],
        compiler_params=pltpu.CompilerParams(
            collective_id=0, has_side_effects=True, vmem_limit_bytes=48 * 2**20
        ),
    )(voltages, *(jnp.asarray(t) for t in tables()))
    return jnp.transpose(products, (0, 2, 1, 3))


def solution(mesh):
    return jax.shard_map(
        local,
        mesh=mesh,
        in_specs=(P(None, "stn", "chan"),),
        out_specs=P("chan", "stn", None, None),
        check_vma=False,
    )
```

time: 969 us -> 242 us (0.25)
  waiting for transfers between devices: 712 us -> 0 us
  Pallas kernels: 0 us -> 234 us
  blocking collectives: 112 us -> 0 us
  starting transfers between devices: 52.7 us -> 0 us
  local copies, waits for them, and re-layouts: 37.1 us -> 7.14 us
  other arithmetic: 28.8 us -> 0 us
  matrix products: 19.8 us -> 0 us
    ppermute x5 -> x0, waiting for transfers between devices: 712 us -> none  [the longest x4 696 us: shifted(): lax.ppermute(array, axis, [(i, (i + by) % count) for i in range(count)])]
    pallas_call x0 -> x1, Pallas kernels: none -> 234 us  [local(): pl.pallas_call(kernel, out_shape=jax.ShapeDtypeStruct((2 * RAD, LAGS, IN_...]
    all_to_all x1 -> x0, blocking collectives: 112 us -> none  [local(): lax.all_to_all(spectra, 'chan', split_axis=0, concat_axis=1, tiled=True)]
    ppermute x5 -> x0, starting transfers between devices: 52.7 us -> none  [the longest x4 47.7 us: shifted(): lax.ppermute(array, axis, [(i, (i + by) % count) for i in range(count)])]
    convert_element_type x3 -> x0, local copies, waits for them, and re-layouts: 23.3 us -> none  [the longest x2 13.8 us: local(): spectra = channelize(filtered, RADIX).astype(jnp.bfloat16)]
    dot_general x7 -> x0, matrix products: 19.8 us -> none  [the longest x1 9.56 us: channelize(): jnp.einsum('ypskb,ybzm->mkszp', turned, block_table(cos_two, sin_two), pr...]
    add x1 -> x0, other arithmetic: 15 us -> none  [local(): filtered + weights[tap_index] * extended[:, :, tap_index:tap_index + per_...]
  transfers between devices with their start and end apart: 5 -> 0, of which waited for: 5 -> 0; matrix products, arithmetic and copies ran while one was open for 1% -> 0% of each run, Pallas kernels for 0% -> 0%
where the time goes in v1:
time: 242 us; the launch traced here: 241 us
  Pallas kernels  234 us (97%)
  local copies, waits for them, and re-layouts  7.14 us (3%)
    pallas_call x1, Pallas kernels, local(): pl.pallas_call(kernel, out_shape=jax.ShapeDtypeStruct((2 * RAD, LAGS, IN_...  234 us
    unnamed x13, local copies, waits for them, and re-layouts  7.14 us

profile of v1, /device:TPU:1, one launch (start us, length us, event | category | flops | bytes accessed | tf_op | source)
XLA Modules:
  0.0 241.2 jit_solution(9580930125314847677)
XLA Ops:
  0.0 0.0 copy-start
  0.0 1.6 copy-done
  1.6 0.0 copy-start.1
  1.6 0.9 copy-done.1
  2.5 0.0 copy-start.2
  2.5 0.8 copy-done.2
  3.3 0.0 copy-start.3
  3.3 0.8 copy-done.3
  4.2 0.0 copy-start.4
  4.2 0.8 copy-done.4
  4.9 0.0 copy-start.5
  4.9 0.7 copy-done.5
  5.7 234.0 %shard_map.64 = bf16[32,5,64,128]{3,2,1,0:T(8,128)(2,1)S(1)} custom-call(bf16[2,64,8192]{2,1,0:T(8,128)(2,1)S(1)} %copy-done, f32[64,128]{1,0:T(8,128)S(1)} %copy-done.4, f32[32,128]{1,0:T(8,128)S(1)} %copy-done.5, bf16[128,256]{1,0:T(8,128)(2,1)S(1)} %copy-done.3, bf16[128,256]{1,0:T(8,128)(2,1)S(1)} %copy-done.2, bf16[256,256]{1,0:T(8,128)(2,1)S(1)} %copy-done.1), custom_call_target="tpu_custom_call" | custom-call | tf_op jit(solution)/shard_map/pallas_call | solution.py:299
  239.7 1.5 copy.8
Async XLA Ops:
  0.0 1.6 copy-start
  1.6 0.9 copy-start.1
  2.5 0.8 copy-start.2
  3.3 0.8 copy-start.3
  4.2 0.8 copy-start.4
  4.9 0.7 copy-start.5

commit v2 on v1

--- a/solution.py
+++ b/solution.py
@@ -23,6 +23,7 @@
 STN = NY * NZH
 LAGS = STN // 2 + 1
 KK = RAD // NY
+TURN = TAPS * RAD
 CHUNKS = 2 * KK
 BF = jnp.bfloat16
 F32 = jnp.float32
@@ -48,7 +49,7 @@
         for j in range(16):
             swap[j, t, t, j] = 1.0
     swap = swap.reshape(256, 256).astype(BF)
-    return weights, twiddle, high, low, swap
+    return np.concatenate([weights, twiddle]), np.concatenate([high, low, swap])
 
 
 def transform(points):
@@ -76,9 +77,9 @@
 
 
 def kernel(
-    x_ref, wts_ref, tw_ref, ah_ref, al_ref, swap_ref, out_ref,
-    halo, yh, yl, b1, r1, zs, zr, gw, ob,
-    halo_send, halo_recv, xy_send, xy_recv, z_send, z_recv, o_send, o_recv,
+    volt_ref, real_ref, half_ref, out_ref,
+    x_ref, real, table, halo, yh, yl, b1, r1, zs, zr, gw, ob,
+    load, halo_send, halo_recv, xy_send, xy_recv, z_send, z_recv, o_send, o_recv,
 ):
     chan, stn = lax.axis_index("chan"), lax.axis_index("stn")
     core = chan % NCORE
@@ -98,6 +99,13 @@
     after = {"chan": (chan + 1) % CHAN, "stn": stn}
     before = {"chan": (chan + CHAN - 1) % CHAN, "stn": stn}
 
+    loads = [
+        pltpu.make_async_copy(src, dst, load.at[i])
+        for i, (src, dst) in enumerate(((volt_ref, x_ref), (real_ref, real), (half_ref, table)))
+    ]
+    for copy in loads:
+        copy.start()
+
     barrier = pltpu.get_barrier_semaphore()
 
     def greet(device):
@@ -118,7 +126,7 @@
 
     def send_halo(block, slot):
         pltpu.make_async_remote_copy(
-            src_ref=x_ref.at[:, :, pl.ds(block * NCH, NCH)],
+            src_ref=volt_ref.at[:, :, pl.ds(block * NCH, NCH)],
             dst_ref=halo.at[slot],
             send_sem=halo_send.at[slot],
             recv_sem=halo_recv.at[slot],
@@ -130,8 +138,8 @@
         pltpu.make_async_copy(halo.at[slot], halo.at[slot], halo_recv.at[slot]).wait()
 
     send_halo(3, 2)
-    send_halo(2, 1)
-    send_halo(1, 0)
+    for copy in loads:
+        copy.wait()
     valid = (chan > 0).astype(F32)
 
     def spectrum(s):
@@ -144,7 +152,7 @@
                 for part in range(2):
                     here = there = None
                     for tap in range(TAPS):
-                        w = wts_ref[pl.ds(tap * RAD + a, 1), :]
+                        w = real[pl.ds(tap * RAD + a, 1), :]
                         j = s - 3 + tap
                         if j >= 0:
                             v = x_ref[part, rows, pl.ds(j * NCH + a * LEN, LEN)].astype(F32) * w
@@ -159,7 +167,7 @@
             for k in range(RAD):
                 re, im = turned[k]
                 if k > 0:
-                    c, sn = tw_ref[pl.ds(k, 1), :], tw_ref[pl.ds(RAD + k, 1), :]
+                    c, sn = real[pl.ds(TURN + k, 1), :], real[pl.ds(TURN + RAD + k, 1), :]
                     re, im = re * c + im * sn, im * c - re * sn
                 re_h, im_h = re.astype(BF), im.astype(BF)
                 re_l = (re - re_h.astype(F32)).astype(BF)
@@ -179,7 +187,7 @@
             k = yd * KK + kk
             for s in range(2):
                 high, low = yh[s, k], yl[s, k]
-                o = dot_nt(ah_ref[...], high) + dot_nt(al_ref[...], high) + dot_nt(ah_ref[...], low)
+                o = dot_nt(table[0:LEN], high) + dot_nt(table[LEN : 2 * LEN], high) + dot_nt(table[0:LEN], low)
                 b1[chunk, pl.ds(yd * NXC, NXC), s] = o.astype(BF).reshape(NXC, 16, LEN)
 
         pltpu.make_async_copy(b1.at[chunk, me_xy], r1.at[chunk, me_xy], xy_recv.at[chunk]).start()
@@ -196,30 +204,48 @@
                 device_id_type=MESH,
             ).start()
 
-    def spread(chunk):
+    def spread(chunk, last=False):
         pltpu.make_async_copy(r1.at[chunk], r1.at[chunk], xy_recv.at[chunk]).wait()
 
         @pl.loop(0, NY)
         def _(yd):
             rows = r1[chunk, pl.ds(yd * NXC, NXC)].reshape(256, LEN)
-            o = jnp.dot(swap_ref[...], rows, preferred_element_type=F32).astype(BF)
+            o = jnp.dot(table[2 * LEN : 4 * LEN], rows, preferred_element_type=F32).astype(BF)
             zs[chunk, :, :, yd] = o.reshape(NZL, 2, 16, LEN)
 
-        pltpu.make_async_copy(zs.at[chunk, zl], zr.at[chunk, me_z], z_recv.at[chunk]).start()
-
-        @pl.loop(1, NZ)
-        def _(j):
-            to = (me_z + j) % NZ
+        def send(part, sem, to):
             pltpu.make_async_remote_copy(
-                src_ref=zs.at[chunk, to % NZL],
-                dst_ref=zr.at[chunk, me_z],
+                src_ref=zs.at[(chunk, to % NZL, *part)],
+                dst_ref=zr.at[(chunk, me_z, *part)],
                 send_sem=z_send,
-                recv_sem=z_recv.at[chunk],
+                recv_sem=sem,
                 device_id=at_z(to),
                 device_id_type=MESH,
             ).start()
 
-    def phase(base):
+        if not last:
+            sem = z_recv.at[chunk]
+            pltpu.make_async_copy(zs.at[chunk, zl], zr.at[chunk, me_z], sem).start()
+
+            @pl.loop(1, NZ)
+            def _(j):
+                send((), sem, (me_z + NZ // 2 + (j // 2) * (1 - 2 * (j % 2)) + NZ) % NZ)
+
+        else:
+            for half in range(2):
+                pltpu.make_async_copy(
+                    zs.at[chunk, zl, half], zr.at[chunk, me_z, half], z_recv.at[chunk + half]
+                ).start()
+            for lo, hi in ((0, 4), (4, NZ)):
+                for half in range(2):
+
+                    @pl.loop(lo, hi)
+                    def _(to, half=half):
+                        @pl.when(to != me_z)
+                        def _():
+                            send((half,), z_recv.at[chunk + half], to)
+
+    def phase(base, last):
         channels(base, 0)
 
         @pl.loop(1, KK)
@@ -227,60 +253,74 @@
             channels(base + kk, kk)
             spread(base + kk - 1)
 
-        spread(base + KK - 1)
+        spread(base + KK - 1, last)
 
     spectrum(3)
     wait_halo(2)
+    send_halo(2, 1)
+    send_halo(1, 0)
     spectrum(2)
-    phase(0)
+    phase(0, False)
     wait_halo(1)
     spectrum(1)
     wait_halo(0)
     spectrum(0)
-    phase(KK)
+    phase(KK, True)
 
     lane = lax.broadcasted_iota(jnp.int32, (IN_DEV, LEN), 1)
     scale = 1.0 / (CHAN * SPEC)
     sign = jnp.where(lane < IN_DEV, scale, -scale).astype(F32)
 
-    @pl.loop(0, KK)
+    def correlate(half, kk):
+        for g in range(STN + LAGS - 1):
+            st = (zh + g) % STN
+            for sp in range(2):
+                part = zr[sp * KK + kk, pl.ds((st % NZH) * NZL, NZL), half, st // NZH]
+                gw[pl.ds(sp * 128, 128), pl.ds(g * LEN, LEN)] = part.reshape(128, LEN)
+        slot = half * KK + kk
+        for yo in range(NY):
+            own = gw[:, pl.ds(2 * yo * LEN, LEN)]
+            partner = gw[:, pl.ds(2 * yo * LEN, LAGS * LEN)]
+            prod = lax.dot_general(
+                own, partner, (((0,), (0,)), ((), ())), preferred_element_type=F32
+            )
+            for lag in range(LAGS):
+                top = prod[:IN_DEV, lag * LEN : (lag + 1) * LEN]
+                low = prod[IN_DEV:, lag * LEN : (lag + 1) * LEN]
+                both = top * sign + pltpu.roll(low, IN_DEV, 1) * scale
+                ob[slot, yo, lag] = both.astype(BF)
+        ch = half * RAD + y * KK + kk
+        pltpu.make_async_copy(ob.at[slot, y], out_ref.at[ch], o_recv).start()
+
+        @pl.loop(1, NY)
+        def _(j):
+            to = (y + j) % NY
+            pltpu.make_async_remote_copy(
+                src_ref=ob.at[slot, to],
+                dst_ref=out_ref.at[ch],
+                send_sem=o_send,
+                recv_sem=o_recv,
+                device_id={"chan": chan, "stn": to * NZH + zh},
+                device_id_type=MESH,
+            ).start()
+
+    def arrived(chunk, *half):
+        here = zr.at[(chunk, slice(None), *half)]
+        pltpu.make_async_copy(here, here, z_recv.at[chunk + sum(half)]).wait()
+
+    @pl.loop(0, KK - 1)
     def _(kk):
-        for base in (0, KK):
-            pltpu.make_async_copy(zr.at[base + kk], zr.at[base + kk], z_recv.at[base + kk]).wait()
+        arrived(kk)
+        arrived(KK + kk)
 
         @pl.loop(0, 2)
         def _(half):
-            for g in range(STN + LAGS - 1):
-                st = (zh + g) % STN
-                for sp in range(2):
-                    part = zr[sp * KK + kk, pl.ds((st % NZH) * NZL, NZL), half, st // NZH]
-                    gw[pl.ds(sp * 128, 128), pl.ds(g * LEN, LEN)] = part.reshape(128, LEN)
-            slot = half * KK + kk
-            for yo in range(NY):
-                own = gw[:, pl.ds(2 * yo * LEN, LEN)]
-                partner = gw[:, pl.ds(2 * yo * LEN, LAGS * LEN)]
-                prod = lax.dot_general(
-                    own, partner, (((0,), (0,)), ((), ())), preferred_element_type=F32
-                )
-                for lag in range(LAGS):
-                    top = prod[:IN_DEV, lag * LEN : (lag + 1) * LEN]
-                    low = prod[IN_DEV:, lag * LEN : (lag + 1) * LEN]
-                    both = top * sign + pltpu.roll(low, IN_DEV, 1) * scale
-                    ob[slot, yo, lag] = both.astype(BF)
-            ch = half * RAD + y * KK + kk
-            pltpu.make_async_copy(ob.at[slot, y], out_ref.at[ch], o_recv).start()
-
-            @pl.loop(1, NY)
-            def _(j):
-                to = (y + j) % NY
-                pltpu.make_async_remote_copy(
-                    src_ref=ob.at[slot, to],
-                    dst_ref=out_ref.at[ch],
-                    send_sem=o_send,
-                    recv_sem=o_recv,
-                    device_id={"chan": chan, "stn": to * NZH + zh},
-                    device_id_type=MESH,
-                ).start()
+            correlate(half, kk)
+
+    arrived(KK - 1)
+    for half in range(2):
+        arrived(CHUNKS - 1, half)
+        correlate(half, KK - 1)
 
     pltpu.make_async_copy(out_ref, out_ref, o_recv).wait()
     for slot in range(3):
@@ -294,14 +334,16 @@
 
 
 def local(voltages):
-    vmem = pl.BlockSpec(memory_space=pltpu.VMEM)
     dma = pltpu.SemaphoreType.DMA
     products = pl.pallas_call(
         kernel,
         out_shape=jax.ShapeDtypeStruct((2 * RAD, LAGS, IN_DEV, LEN), BF),
-        in_specs=[vmem] * 6,
+        in_specs=[pl.BlockSpec(memory_space=pl.ANY)] * 3,
         out_specs=pl.BlockSpec(memory_space=pl.ANY),
         scratch_shapes=[
+            pltpu.VMEM((2, IN_DEV, SPEC * NCH), BF),
+            pltpu.VMEM((TURN + 2 * RAD, LEN), F32),
+            pltpu.VMEM((4 * LEN, 2 * LEN), BF),
             pltpu.VMEM((3, 2, IN_DEV, NCH), BF),
             pltpu.VMEM((2, RAD, 2 * IN_DEV, 2 * LEN), BF),
             pltpu.VMEM((2, RAD, 2 * IN_DEV, 2 * LEN), BF),
@@ -313,15 +355,16 @@
             pltpu.VMEM((2 * KK, NY, LAGS, IN_DEV, LEN), BF),
             dma((3,)),
             dma((3,)),
+            dma((3,)),
             dma,
             dma((CHUNKS,)),
             dma,
-            dma((CHUNKS,)),
+            dma((CHUNKS + 1,)),
             dma,
             dma,
         ],
         compiler_params=pltpu.CompilerParams(
-            collective_id=0, has_side_effects=True, vmem_limit_bytes=48 * 2**20
+            collective_id=0, has_side_effects=True, vmem_limit_bytes=60 * 2**20
         ),
     )(voltages, *(jnp.asarray(t) for t in tables()))
     return jnp.transpose(products, (0, 2, 1, 3))

time: 242 us -> 227 us (0.938)
  the two profiles are of different devices: /device:TPU:1 before, /device:TPU:128 now
where the time goes in v2:
time: 227 us
  Pallas kernels  223 us (98%)
  local copies, waits for them, and re-layouts  3.82 us (2%)
    pallas_call x1, Pallas kernels, local(): pl.pallas_call(kernel, out_shape=jax.ShapeDtypeStruct((2 * RAD, LAGS, IN_...  223 us

profile of v2, /device:TPU:128, one launch (start us, length us, event | category | flops | bytes accessed | tf_op | source)
XLA Modules:
  0.0 227.1 jit_solution(2448138814709346934)
XLA Ops:
  0.0 223.3 %shard_map.37 = bf16[32,5,64,128]{3,2,1,0:T(8,128)(2,1)} custom-call(bf16[2,64,8192]{2,1,0:T(8,128)(2,1)} %volt_ref.1, f32[96,128]{1,0:T(8,128)} %constant.4.clone.real_ref, bf16[512,256]{1,0:T(8,128)(2,1)} %constant.5.clone.half_ref), custom_call_target="tpu_custom_call" | custom-call | tf_op jit(solution)/shard_map/pallas_call | solution.py:338
  223.3 3.8 %copy.5 = bf16[32,64,5,128]{3,1,2,0:T(8,128)(2,1)} copy(bf16[32,64,5,128]{3,1,2,0:T(8,128)(2,1)} %bitcast.1) | data formatting | bytes 5242880

commit v3 on v2

--- a/solution.py
+++ b/solution.py
@@ -114,13 +114,13 @@
     greet(after)
     greet(before)
 
+    @pl.loop(1, NZ)
+    def _(j):
+        greet(at_z((me_z + j) % NZ))
+
     @pl.loop(1, PLANE)
     def _(j):
         greet(at_xy((me_xy + j) % PLANE))
-
-    @pl.loop(1, NZ)
-    def _(j):
-        greet(at_z((me_z + j) % NZ))
 
     pl.semaphore_wait(barrier, PLANE + NZ)
 
@@ -181,91 +181,105 @@
     def dot_nt(a, b):
         return lax.dot_general(a, b, (((1,), (1,)), ((), ())), preferred_element_type=F32)
 
-    def channels(chunk, kk):
+    def channels(chunk):
         @pl.loop(0, NY)
         def _(yd):
-            k = yd * KK + kk
+            k = yd * KK + chunk % KK
             for s in range(2):
                 high, low = yh[s, k], yl[s, k]
                 o = dot_nt(table[0:LEN], high) + dot_nt(table[LEN : 2 * LEN], high) + dot_nt(table[0:LEN], low)
                 b1[chunk, pl.ds(yd * NXC, NXC), s] = o.astype(BF).reshape(NXC, 16, LEN)
 
-        pltpu.make_async_copy(b1.at[chunk, me_xy], r1.at[chunk, me_xy], xy_recv.at[chunk]).start()
+    def trade(first, count, sem):
+        some = pl.ds(first, count)
+        pltpu.make_async_copy(b1.at[some, me_xy], r1.at[some, me_xy], sem).start()
 
         @pl.loop(1, PLANE)
         def _(j):
             to = (me_xy + j) % PLANE
             pltpu.make_async_remote_copy(
-                src_ref=b1.at[chunk, to],
-                dst_ref=r1.at[chunk, me_xy],
+                src_ref=b1.at[some, to],
+                dst_ref=r1.at[some, me_xy],
                 send_sem=xy_send,
-                recv_sem=xy_recv.at[chunk],
+                recv_sem=sem,
                 device_id=at_xy(to),
                 device_id_type=MESH,
             ).start()
 
-    def spread(chunk, last=False):
-        pltpu.make_async_copy(r1.at[chunk], r1.at[chunk], xy_recv.at[chunk]).wait()
-
+    def traded(first, count, sem):
+        here = r1.at[pl.ds(first, count)]
+        pltpu.make_async_copy(here, here, sem).wait()
+
+    def spread(chunk):
         @pl.loop(0, NY)
         def _(yd):
             rows = r1[chunk, pl.ds(yd * NXC, NXC)].reshape(256, LEN)
             o = jnp.dot(table[2 * LEN : 4 * LEN], rows, preferred_element_type=F32).astype(BF)
             zs[chunk, :, :, yd] = o.reshape(NZL, 2, 16, LEN)
 
-        def send(part, sem, to):
-            pltpu.make_async_remote_copy(
-                src_ref=zs.at[(chunk, to % NZL, *part)],
-                dst_ref=zr.at[(chunk, me_z, *part)],
-                send_sem=z_send,
-                recv_sem=sem,
-                device_id=at_z(to),
-                device_id_type=MESH,
-            ).start()
-
-        if not last:
-            sem = z_recv.at[chunk]
-            pltpu.make_async_copy(zs.at[chunk, zl], zr.at[chunk, me_z], sem).start()
-
-            @pl.loop(1, NZ)
-            def _(j):
-                send((), sem, (me_z + NZ // 2 + (j // 2) * (1 - 2 * (j % 2)) + NZ) % NZ)
-
-        else:
+    def send(chunks, part, sem, to):
+        pltpu.make_async_remote_copy(
+            src_ref=zs.at[(chunks, to % NZL, *part)],
+            dst_ref=zr.at[(chunks, me_z, *part)],
+            send_sem=z_send,
+            recv_sem=sem,
+            device_id=at_z(to),
+            device_id_type=MESH,
+        ).start()
+
+    def pass_on(first, count, sem):
+        some = pl.ds(first, count)
+        pltpu.make_async_copy(zs.at[some, zl], zr.at[some, me_z], sem).start()
+
+        @pl.loop(1, NZ)
+        def _(j):
+            send(some, (), sem, (me_z + NZ // 2 + (j // 2) * (1 - 2 * (j % 2)) * (1 - 2 * core) + NZ) % NZ)
+
+    def pass_last(chunk, sems):
+        for half in range(2):
+            pltpu.make_async_copy(zs.at[chunk, zl, half], zr.at[chunk, me_z, half], sems[half]).start()
+        for lo, hi in ((0, 4), (4, NZ)):
             for half in range(2):
-                pltpu.make_async_copy(
-                    zs.at[chunk, zl, half], zr.at[chunk, me_z, half], z_recv.at[chunk + half]
-                ).start()
-            for lo, hi in ((0, 4), (4, NZ)):
-                for half in range(2):
-
-                    @pl.loop(lo, hi)
-                    def _(to, half=half):
-                        @pl.when(to != me_z)
-                        def _():
-                            send((half,), z_recv.at[chunk + half], to)
-
-    def phase(base, last):
-        channels(base, 0)
-
-        @pl.loop(1, KK)
-        def _(kk):
-            channels(base + kk, kk)
-            spread(base + kk - 1)
-
-        spread(base + KK - 1, last)
+
+                @pl.loop(lo, hi)
+                def _(to, half=half):
+                    @pl.when(to != me_z)
+                    def _():
+                        send(chunk, (half,), sems[half], to)
+
+    def arrived(sem, chunks, *half):
+        here = zr.at[(chunks, slice(None), *half)]
+        pltpu.make_async_copy(here, here, sem).wait()
+
+    def some(first, count, step):
+        pl.loop(first, first + count)(step)
 
     spectrum(3)
     wait_halo(2)
     send_halo(2, 1)
     send_halo(1, 0)
     spectrum(2)
-    phase(0, False)
+    channels(0)
+    trade(0, 1, xy_recv.at[0])
+    some(1, KK - 1, channels)
+    trade(1, KK - 1, xy_recv.at[1])
+    traded(0, 1, xy_recv.at[0])
+    spread(0)
+    pass_on(0, 1, z_recv.at[0])
+    traded(1, KK - 1, xy_recv.at[1])
+    some(1, KK - 1, spread)
+    pass_on(1, KK - 1, z_recv.at[1])
     wait_halo(1)
     spectrum(1)
     wait_halo(0)
     spectrum(0)
-    phase(KK, True)
+    some(KK, KK, channels)
+    trade(KK, KK, xy_recv.at[2])
+    traded(KK, KK, xy_recv.at[2])
+    some(KK, KK, spread)
+    pass_on(KK, 2, z_recv.at[2])
+    pass_on(KK + 2, 1, z_recv.at[3])
+    pass_last(CHUNKS - 1, (z_recv.at[4], z_recv.at[5]))
 
     lane = lax.broadcasted_iota(jnp.int32, (IN_DEV, LEN), 1)
     scale = 1.0 / (CHAN * SPEC)
@@ -278,23 +292,26 @@
                 part = zr[sp * KK + kk, pl.ds((st % NZH) * NZL, NZL), half, st // NZH]
                 gw[pl.ds(sp * 128, 128), pl.ds(g * LEN, LEN)] = part.reshape(128, LEN)
         slot = half * KK + kk
-        for yo in range(NY):
-            own = gw[:, pl.ds(2 * yo * LEN, LEN)]
-            partner = gw[:, pl.ds(2 * yo * LEN, LAGS * LEN)]
+        ch = half * RAD + y * KK + kk
+
+        def products(to):
+            at = pl.multiple_of(2 * to * LEN, LEN)
             prod = lax.dot_general(
-                own, partner, (((0,), (0,)), ((), ())), preferred_element_type=F32
+                gw[:, pl.ds(at, LEN)],
+                gw[:, pl.ds(at, LAGS * LEN)],
+                (((0,), (0,)), ((), ())),
+                preferred_element_type=F32,
             )
             for lag in range(LAGS):
                 top = prod[:IN_DEV, lag * LEN : (lag + 1) * LEN]
                 low = prod[IN_DEV:, lag * LEN : (lag + 1) * LEN]
-                both = top * sign + pltpu.roll(low, IN_DEV, 1) * scale
-                ob[slot, yo, lag] = both.astype(BF)
-        ch = half * RAD + y * KK + kk
-        pltpu.make_async_copy(ob.at[slot, y], out_ref.at[ch], o_recv).start()
-
-        @pl.loop(1, NY)
+                whole = top * sign + pltpu.roll(low, IN_DEV, 1) * scale
+                ob[slot, to, lag] = whole.astype(BF)
+
+        @pl.loop(0, NY - 1)
         def _(j):
-            to = (y + j) % NY
+            to = (y + (j + 1) % (NY - 1) + 1) % NY
+            products(to)
             pltpu.make_async_remote_copy(
                 src_ref=ob.at[slot, to],
                 dst_ref=out_ref.at[ch],
@@ -304,22 +321,20 @@
                 device_id_type=MESH,
             ).start()
 
-    def arrived(chunk, *half):
-        here = zr.at[(chunk, slice(None), *half)]
-        pltpu.make_async_copy(here, here, z_recv.at[chunk + sum(half)]).wait()
-
-    @pl.loop(0, KK - 1)
-    def _(kk):
-        arrived(kk)
-        arrived(KK + kk)
-
-        @pl.loop(0, 2)
-        def _(half):
-            correlate(half, kk)
-
-    arrived(KK - 1)
+        products(y)
+        pltpu.make_async_copy(ob.at[slot, y], out_ref.at[ch], o_recv).start()
+
+    def both(kk):
+        pl.loop(0, 2)(lambda half: correlate(half, kk))
+
+    arrived(z_recv.at[0], 0)
+    arrived(z_recv.at[1], pl.ds(1, KK - 1))
+    arrived(z_recv.at[2], pl.ds(KK, 2))
+    some(0, 2, both)
+    arrived(z_recv.at[3], KK + 2)
+    both(2)
     for half in range(2):
-        arrived(CHUNKS - 1, half)
+        arrived(z_recv.at[4 + half], CHUNKS - 1, half)
         correlate(half, KK - 1)
 
     pltpu.make_async_copy(out_ref, out_ref, o_recv).wait()
@@ -331,6 +346,17 @@
     pltpu.make_async_copy(sent, sent, z_send).wait()
     sent = ob.at[:, pl.ds(0, NY - 1)]
     pltpu.make_async_copy(sent, sent, o_send).wait()
+
+
+def finish(src, dst, held, sems, more):
+    parts = [pl.ds(8 * i, 8) for i in range(4)]
+    for i, part in enumerate(parts):
+        pltpu.make_async_copy(src.at[part], held.at[part], sems.at[i]).start()
+    for i, part in enumerate(parts):
+        pltpu.make_async_copy(src.at[part], held.at[part], sems.at[i]).wait()
+        pltpu.make_async_copy(held.at[part], dst.at[part], more.at[i]).start()
+    for i, part in enumerate(parts):
+        pltpu.make_async_copy(held.at[part], dst.at[part], more.at[i]).wait()
 
 
 def local(voltages):
@@ -357,9 +383,9 @@
             dma((3,)),
             dma((3,)),
             dma,
-            dma((CHUNKS,)),
+            dma((3,)),
             dma,
-            dma((CHUNKS + 1,)),
+            dma((6,)),
             dma,
             dma,
         ],
@@ -367,6 +393,14 @@
             collective_id=0, has_side_effects=True, vmem_limit_bytes=60 * 2**20
         ),
     )(voltages, *(jnp.asarray(t) for t in tables()))
+    products = pl.pallas_call(
+        finish,
+        out_shape=jax.ShapeDtypeStruct((2 * RAD, LAGS, IN_DEV, LEN), BF),
+        in_specs=[pl.BlockSpec(memory_space=pl.ANY)],
+        out_specs=pl.BlockSpec(memory_space=pl.ANY),
+        scratch_shapes=[pltpu.VMEM((2 * RAD, LAGS, IN_DEV, LEN), BF), dma((4,)), dma((4,))],
+        compiler_params=pltpu.CompilerParams(vmem_limit_bytes=60 * 2**20),
+    )(products)
     return jnp.transpose(products, (0, 2, 1, 3))
 
 

time: 227 us -> 226 us (level)
  the two profiles are of different devices: /device:TPU:128 before, /device:TPU:131 now
where the time goes in v3:
time: 226 us
  Pallas kernels  226 us (100%)
    pallas_call x1, Pallas kernels, local(): pl.pallas_call(kernel, out_shape=jax.ShapeDtypeStruct((2 * RAD, LAGS, IN_...  223 us

profile of v3, /device:TPU:131, one launch (start us, length us, event | category | flops | bytes accessed | tf_op | source)
XLA Modules:
  0.0 225.7 jit_solution(18127950523392737290)
XLA Ops:
  0.0 223.1 %shard_map.37.src = bf16[32,5,64,128]{3,2,1,0:T(8,128)(2,1)} custom-call(bf16[2,64,8192]{2,1,0:T(8,128)(2,1)} %volt_ref.1, f32[96,128]{1,0:T(8,128)} %constant.4.clone.real_ref, bf16[512,256]{1,0:T(8,128)(2,1)} %constant.5.clone.half_ref), custom_call_target="tpu_custom_call" | custom-call | tf_op jit(solution)/shard_map/pallas_call | solution.py:364
  223.1 2.6 %shard_map.38 = bf16[32,5,64,128]{3,2,1,0:T(8,128)(2,1)} custom-call(bf16[32,5,64,128]{3,2,1,0:T(8,128)(2,1)} %shard_map.37.src), custom_call_target="tpu_custom_call" | custom-call | tf_op jit(solution)/shard_map/pallas_call | solution.py:396

commit v4 on v3

--- a/solution.py
+++ b/solution.py
@@ -181,11 +181,11 @@
     def dot_nt(a, b):
         return lax.dot_general(a, b, (((1,), (1,)), ((), ())), preferred_element_type=F32)
 
-    def channels(chunk):
+    def channels(chunk, *parts):
         @pl.loop(0, NY)
         def _(yd):
             k = yd * KK + chunk % KK
-            for s in range(2):
+            for s in parts:
                 high, low = yh[s, k], yl[s, k]
                 o = dot_nt(table[0:LEN], high) + dot_nt(table[LEN : 2 * LEN], high) + dot_nt(table[0:LEN], low)
                 b1[chunk, pl.ds(yd * NXC, NXC), s] = o.astype(BF).reshape(NXC, 16, LEN)
@@ -242,7 +242,9 @@
             for half in range(2):
 
                 @pl.loop(lo, hi)
-                def _(to, half=half):
+                def _(j, lo=lo, hi=hi, half=half):
+                    to = j + core * (hi + lo - 1 - 2 * j)
+
                     @pl.when(to != me_z)
                     def _():
                         send(chunk, (half,), sems[half], to)
@@ -255,17 +257,18 @@
         pl.loop(first, first + count)(step)
 
     spectrum(3)
+    some(0, KK, lambda chunk: channels(chunk, 1))
     wait_halo(2)
     send_halo(2, 1)
     send_halo(1, 0)
     spectrum(2)
-    channels(0)
+    channels(0, 0)
     trade(0, 1, xy_recv.at[0])
-    some(1, KK - 1, channels)
-    trade(1, KK - 1, xy_recv.at[1])
     traded(0, 1, xy_recv.at[0])
     spread(0)
     pass_on(0, 1, z_recv.at[0])
+    some(1, KK - 1, lambda chunk: channels(chunk, 0))
+    trade(1, KK - 1, xy_recv.at[1])
     traded(1, KK - 1, xy_recv.at[1])
     some(1, KK - 1, spread)
     pass_on(1, KK - 1, z_recv.at[1])
@@ -273,7 +276,7 @@
     spectrum(1)
     wait_halo(0)
     spectrum(0)
-    some(KK, KK, channels)
+    some(KK, KK, lambda chunk: channels(chunk, 0, 1))
     trade(KK, KK, xy_recv.at[2])
     traded(KK, KK, xy_recv.at[2])
     some(KK, KK, spread)

time: 226 us -> 226 us (level)
  the two profiles are of different devices: /device:TPU:131 before, /device:TPU:1 now
where the time goes in v4:
time: 226 us; the launch traced here: 222 us
  Pallas kernels  222 us (98%)
    pallas_call x1, Pallas kernels, local(): pl.pallas_call(kernel, out_shape=jax.ShapeDtypeStruct((2 * RAD, LAGS, IN_...  220 us

profile of v4, /device:TPU:1, one launch (start us, length us, event | category | flops | bytes accessed | tf_op | source)
XLA Modules:
  0.0 222.3 jit_solution(6816081402437210321)
XLA Ops:
  0.0 219.7 %shard_map.37.src = bf16[32,5,64,128]{3,2,1,0:T(8,128)(2,1)} custom-call(bf16[2,64,8192]{2,1,0:T(8,128)(2,1)} %volt_ref.1, f32[96,128]{1,0:T(8,128)} %constant.4.clone.real_ref, bf16[512,256]{1,0:T(8,128)(2,1)} %constant.5.clone.half_ref), custom_call_target="tpu_custom_call" | custom-call | tf_op jit(solution)/shard_map/pallas_call | solution.py:367
  219.7 2.6 %shard_map.38 = bf16[32,5,64,128]{3,2,1,0:T(8,128)(2,1)} custom-call(bf16[32,5,64,128]{3,2,1,0:T(8,128)(2,1)} %shard_map.37.src), custom_call_target="tpu_custom_call" | custom-call | tf_op jit(solution)/shard_map/pallas_call | solution.py:399

commit v5 on v4

--- a/solution.py
+++ b/solution.py
@@ -125,19 +125,28 @@
     pl.semaphore_wait(barrier, PLANE + NZ)
 
     def send_halo(block, slot):
-        pltpu.make_async_remote_copy(
-            src_ref=volt_ref.at[:, :, pl.ds(block * NCH, NCH)],
-            dst_ref=halo.at[slot],
-            send_sem=halo_send.at[slot],
-            recv_sem=halo_recv.at[slot],
-            device_id=after,
-            device_id_type=MESH,
-        ).start()
+        @pl.when(chan < CHAN - 1)
+        def _():
+            pltpu.make_async_remote_copy(
+                src_ref=volt_ref.at[:, :, pl.ds(block * NCH, NCH)],
+                dst_ref=halo.at[slot],
+                send_sem=halo_send.at[slot],
+                recv_sem=halo_recv.at[slot],
+                device_id=after,
+                device_id_type=MESH,
+            ).start()
 
     def wait_halo(slot):
-        pltpu.make_async_copy(halo.at[slot], halo.at[slot], halo_recv.at[slot]).wait()
+        @pl.when(chan > 0)
+        def _():
+            pltpu.make_async_copy(halo.at[slot], halo.at[slot], halo_recv.at[slot]).wait()
 
     send_halo(3, 2)
+
+    @pl.when(chan == 0)
+    def _():
+        halo[...] = jnp.zeros_like(halo)
+
     for copy in loads:
         copy.wait()
     valid = (chan > 0).astype(F32)
@@ -341,8 +350,12 @@
         correlate(half, KK - 1)
 
     pltpu.make_async_copy(out_ref, out_ref, o_recv).wait()
-    for slot in range(3):
-        pltpu.make_async_copy(halo.at[slot], halo.at[slot], halo_send.at[slot]).wait()
+
+    @pl.when(chan < CHAN - 1)
+    def _():
+        for slot in range(3):
+            pltpu.make_async_copy(halo.at[slot], halo.at[slot], halo_send.at[slot]).wait()
+
     sent = b1.at[:, pl.ds(0, PLANE - 1)]
     pltpu.make_async_copy(sent, sent, xy_send).wait()
     sent = zr.at[:, pl.ds(0, NZ - 1)]

time: 226 us -> 226 us (level)
  no operation moved by 1% of the time
where the time goes in v5:
time: 226 us; the launch traced here: 222 us
  Pallas kernels  222 us (98%)
    pallas_call x1, Pallas kernels, local(): pl.pallas_call(kernel, out_shape=jax.ShapeDtypeStruct((2 * RAD, LAGS, IN_...  220 us

profile of v5, /device:TPU:1, one launch (start us, length us, event | category | flops | bytes accessed | tf_op | source)
XLA Modules:
  0.0 222.3 jit_solution(6750771466141855230)
XLA Ops:
  0.0 219.7 %shard_map.37.src = bf16[32,5,64,128]{3,2,1,0:T(8,128)(2,1)} custom-call(bf16[2,64,8192]{2,1,0:T(8,128)(2,1)} %volt_ref.1, f32[96,128]{1,0:T(8,128)} %constant.4.clone.real_ref, bf16[512,256]{1,0:T(8,128)(2,1)} %constant.5.clone.half_ref), custom_call_target="tpu_custom_call" | custom-call | tf_op jit(solution)/shard_map/pallas_call | solution.py:380
  219.7 2.6 %shard_map.38 = bf16[32,5,64,128]{3,2,1,0:T(8,128)(2,1)} custom-call(bf16[32,5,64,128]{3,2,1,0:T(8,128)(2,1)} %shard_map.37.src), custom_call_target="tpu_custom_call" | custom-call | tf_op jit(solution)/shard_map/pallas_call | solution.py:412
